TPU v7x, 512 devices: a whole 4x4x16 slice. The times are simulated.
512 devices in a mesh: prow: 16 (over z), pcol: 32 (over x, y, core).
Axes of the slice: x: 4, y: 4, z: 16, core: 2. Of those that a mesh axis runs over, the one named last changes fastest.
Arguments:
- matrix: float32 [8192, 8192], P('prow', 'pcol'), may hold values from -6 to 6
- factored_panel: float32 [8192, 256], P('prow', 'pcol')
- pivots: int32 [256], replicated, may hold values from 0 to 8191, as said below
Outputs:
- updated: float32 [8192, 8192], P('prow', 'pcol')
Inputs may be any that keep to these rules, and one draw needn't show every extreme that they name: pivots[j] is j or larger for every j; 8191 appears among the entries.
All inputs are finite; a program needn't handle non-finite values.
Results may differ from a plain program's by a relative error of at most 0.000055.
Values sent between devices are 32-bit elements; how exact they have to be, the bound alone decides.
No kernel may reach another device: no remote copies, remote signals or barrier semaphores. Data moves between devices by JAX's collectives and lax.ppermute only.
A program may use at most 64 MiB of HBM per device.

v0:
```python
from functools import partial

import jax
import jax.numpy as jnp
from jax import lax
from jax.sharding import PartitionSpec as P


def spread(value, axis, source):
    kept = jnp.where(lax.axis_index(axis) == source, value, 0).astype(value.dtype)
    return lax.psum(kept, axis)


def exchange_rows(pivots, column, row_order):
    target = pivots[column]
    first = row_order[column]
    second = row_order[target]
    return row_order.at[column].set(second).at[target].set(first)


def unit_lower(diagonal):
    size_nb = diagonal.shape[0]
    return jnp.tril(diagonal, -1) + jnp.eye(size_nb, dtype=jnp.float32)


def tri_solve(lower_tri, right_rows):
    return jax.scipy.linalg.solve_triangular(lower_tri, right_rows, lower=True, unit_diagonal=True)


def local(matrix, factored_panel, pivots):
    row_count = matrix.shape[0]
    panel_width = pivots.shape[0]
    proc_row = lax.axis_index("prow")
    all_rows = row_count * lax.axis_size("prow")
    row_order = lax.fori_loop(
        0, panel_width, partial(exchange_rows, pivots), jnp.arange(all_rows, dtype=jnp.int32)
    )
    local_idx = row_order[:panel_width] - proc_row * row_count
    owned_rows = (local_idx >= 0) & (local_idx < row_count)
    chosen = jnp.where(owned_rows[:, None], matrix[jnp.clip(local_idx, 0, row_count - 1)], 0.0)
    upper_source = lax.psum(chosen, "prow")
    leading = spread(matrix[:panel_width], "prow", 0)
    global_rows = proc_row * row_count + jnp.arange(row_count, dtype=jnp.int32)
    source = lax.dynamic_slice_in_dim(row_order, proc_row * row_count, row_count)
    incoming = leading[jnp.clip(source, 0, panel_width - 1)]
    swapped = jnp.where((source == global_rows)[:, None], matrix, incoming)
    diagonal = lax.all_gather(factored_panel[:panel_width], "pcol", axis=1, tiled=True)
    identity_nb = jnp.eye(panel_width, dtype=jnp.float32)
    lower_tri = jnp.where(proc_row == 0, unit_lower(diagonal), identity_nb)
    upper_rows = spread(tri_solve(lower_tri, upper_source), "prow", 0)
    whole_panel = lax.all_gather(factored_panel, "pcol", axis=1, tiled=True)
    updated = swapped - jnp.dot(
        whole_panel, upper_rows, precision=lax.Precision.HIGHEST, preferred_element_type=jnp.float32
    )
    top_block = jnp.where(proc_row == 0, upper_rows, updated[:panel_width])
    return jnp.concatenate([top_block, updated[panel_width:]], axis=0)


def solution(mesh):
    return jax.shard_map(
        local,
        mesh=mesh,
        in_specs=(P("prow", "pcol"), P("prow", "pcol"), P()),
        out_specs=P("prow", "pcol"),
        check_vma=False,
    )
```

profile of v0, /device:TPU:1, one launch (start us, length us, event | category | flops | bytes accessed | tf_op | source)
XLA Modules:
  0.0 1430.5 jit_solution(12192892985408474421)
XLA Ops:
  7.2 1141.0 %while.16 = (s32[]{:T(128)}, s32[8192]{0:T(1024)S(1)}, s32[256]{0:T(256)S(1)}, s32[]{:T(128)}, s32[]{:T(128)}, /*index=5*/s32[]{:T(128)}, s32[]{:T(128)}) while((s32[]{:T(128)}, s32[8192]{0:T(1024)S(1)}, s32[256]{0:T(256)S(1)}, s32[]{:T(128)}, s32[]{:T(128)}, /*index=5*/s32[]{:T(128)}, s32[]{:T(128)}) %tuple.73), condition=%wide.region_1.2_spmd, body=%wide.region_0.1_spmd.sunk | while | flops 13 | bytes 2255 | solution.py:35
  10.0 0.8 select_dynamic-update-slice_fusion.4
  23.4 0.8 select_dynamic-update-slice_fusion.4
  27.9 0.8 select_dynamic-update-slice_fusion.4
  54.6 0.8 select_dynamic-update-slice_fusion.4
  68.0 0.8 select_dynamic-update-slice_fusion.4
  72.4 0.8 select_dynamic-update-slice_fusion.4
  90.2 0.8 select_dynamic-update-slice_fusion.4
  94.7 0.8 select_dynamic-update-slice_fusion.4
  108.1 0.8 select_dynamic-update-slice_fusion.4
  112.5 0.8 select_dynamic-update-slice_fusion.4
  125.9 0.8 select_dynamic-update-slice_fusion.4
  139.3 0.8 select_dynamic-update-slice_fusion.4
  143.7 0.8 select_dynamic-update-slice_fusion.4
  157.1 0.8 select_dynamic-update-slice_fusion.4
  161.6 0.8 select_dynamic-update-slice_fusion.4
  174.9 0.8 select_dynamic-update-slice_fusion.4
  179.4 0.8 select_dynamic-update-slice_fusion.4
  192.8 0.8 select_dynamic-update-slice_fusion.4
  197.2 0.8 select_dynamic-update-slice_fusion.4
  1148.3 2.0 gather_fusion
  1151.2 28.7 %all_gather.6 = f32[256,256]{0,1:T(8,128)S(1)} all-gather(f32[256,8]{0,1:T(8,128)S(1)} %slice-done), channel_id=1, replica_groups=mesh['prow'=16,'pcol'=32] {'pcol'}, dimensions={1}, use_global_device_ids=true | all-gather | bytes 270336 | tf_op jit(solution)/shard_map/all_gather | solution.py:47
  1180.8 4.1 while.17
  1181.5 1.4 bitcast_dynamic-update-slice_fusion.2
  1183.5 1.4 bitcast_dynamic-update-slice_fusion.2
  1184.9 19.7 %custom-call.4 = f32[2,128,128]{1,2,0:T(8,128)S(1)} custom-call(f32[2,128,128]{2,1,0:T(8,128)S(1)} %get-tuple-element.121), custom_call_target="InvertDiagBlocksLowerTriangular" | custom-call | tf_op jit(solution)/shard_map/jit(_solve_triangular)/triangular_solve | solution.py:27
  1204.6 78.4 %all-reduce.4.cloned.1.call-done = f32[256,256]{1,0:T(8,128)} async-done(((f32[256,256]{1,0:T(8,128)}), f32[256,256]{1,0:T(8,128)}) %all-reduce.4.cloned.1.call-update) | async-done | bytes 262160 | tf_op jit(solution)/shard_map/psum | solution.py:41
  1283.0 1.3 fusion.3
  1286.3 34.5 %all_gather.7 = f32[512,256]{0,1:T(8,128)S(1)} all-gather(f32[512,8]{0,1:T(8,128)S(1)} %copy-done.3), channel_id=1, replica_groups=mesh['prow'=16,'pcol'=32] {'pcol'}, dimensions={1}, use_global_device_ids=true | all-gather | bytes 540672 | tf_op jit(solution)/shard_map/all_gather | solution.py:51
  1320.9 98.3 %all-reduce.6.cloned.1.call-done = (f32[256,256]{1,0:T(8,128)}, f32[256,256]{1,0:T(8,128)}) async-done(((f32[256,256]{1,0:T(8,128)}, f32[256,256]{1,0:T(8,128)}), (f32[256,256]{1,0:T(8,128)}, f32[256,256]{1,0:T(8,128)})) %all-reduce.6.cloned.1.call-update) | async-done | bytes 524304 | tf_op jit(solution)/shard_map/psum | solution.py:11
  1419.2 2.6 gather_fusion.1
  1421.7 1.0 fusion
  (1046 shorter events, 709.5 us)
Async XLA Ops:
  6.5 1276.5 %all-reduce.4.cloned.1.call-start = ((), (), s32[]{:S(2)}) async-start(), calls=%async_computation | async-start | bytes 524288 | tf_op jit(solution)/shard_map/psum | solution.py:41
  6.5 0.7 copy-start.5
  1150.3 0.9 slice-start
  1151.1 28.9 %copy-start = (f32[512,256]{1,0:T(8,128)S(1)}, f32[512,256]{1,0:T(8,128)}, u32[]{:S(2)}) copy-start(f32[512,256]{1,0:T(8,128)} %param.9) | copy-start | bytes 1572868
  1151.1 268.1 %all-reduce.6.cloned.1.call-start = ((), (), s32[]{:S(2)}) async-start(), calls=%async_computation.1 | async-start | bytes 1048576 | tf_op jit(solution)/shard_map/psum | solution.py:11
  1283.0 1.3 copy-start.2
  1285.6 0.7 copy-start.3
  1419.2 2.6 copy-start.1
  1422.8 0.8 copy-start.4
Sparse Core Ops, SparseCore 0:
  1151.2 131.7 all-reduce.3
  1285.7 133.3 all-reduce.5
where the time goes:
time: 1450 us; the launch traced here: 1430 us
  other arithmetic  445 us (31%)
  loops' own time  423 us (29%)
  local copies, waits for them, and re-layouts  307 us (21%)
  waiting for transfers between devices  177 us (12%)
  blocking collectives  63.2 us (4%)
    another operation x1, loops' own time, local(): lax.fori_loop(0, panel_width, partial(exchange_rows, pivots), jnp.arange(...  423 us
    scatter x512, other arithmetic, exchange_rows(): return row_order.at[column].set(second).at[target].set(first)  422 us
    another operation x262, local copies, waits for them, and re-layouts  159 us
    dynamic_slice x256, local copies, waits for them, and re-layouts, exchange_rows(): target = pivots[column]  141 us
    psum x1, waiting for transfers between devices, spread(): return lax.psum(kept, axis)  98.3 us
    psum x1, waiting for transfers between devices, local(): upper_source = lax.psum(chosen, 'prow')  78.4 us
    all_gather x1, blocking collectives, local(): whole_panel = lax.all_gather(factored_panel, 'pcol', axis=1, tiled=True)  34.5 us
  transfers between devices with their start and end apart: 2, of which 2 were waited for; matrix products, arithmetic and copies ran while one was open for 2% of the time, Pallas kernels for 0%

commit v1 on v0

v1 whole, which is shorter than its diff:
```python
import jax
import jax.numpy as jnp
from jax import lax
from jax.experimental import pallas as pl
from jax.experimental.pallas import tpu as pltpu
from jax.sharding import PartitionSpec as P

HIGHEST = lax.Precision.HIGHEST
VMEM = pl.BlockSpec(memory_space=pltpu.VMEM)
SMEM = pl.BlockSpec(memory_space=pltpu.SMEM)


def dot_lhs_t(a, b):
    return lax.dot_general(
        a, b, (((0,), (0,)), ((), ())), precision=HIGHEST, preferred_element_type=jnp.float32
    )


def dot(a, b):
    return jnp.dot(a, b, precision=HIGHEST, preferred_element_type=jnp.float32)


def pack_kernel(pivots_ref, matrix_ref, panel_ref, send_ref, table_ref, order_ref):
    nb = pivots_ref.shape[0]
    rows = matrix_ref.shape[0]
    slots = nb // send_ref.shape[0]
    me = lax.axis_index("prow")

    def start(j, _):
        target = pivots_ref[j]
        order_ref[target] = target
        order_ref[j] = j
        return 0

    lax.fori_loop(0, nb, start, 0, unroll=8)

    def exchange(j, _):
        target = pivots_ref[j]
        first = order_ref[j]
        second = order_ref[target]
        order_ref[j] = second
        order_ref[target] = first
        return 0

    lax.fori_loop(0, nb, exchange, 0, unroll=8)

    def place(i, count):
        row = order_ref[i]
        partner = order_ref[row]
        table_ref[i] = row
        table_ref[nb + i] = partner
        mine = row - me * rows
        owned = (mine >= 0) & (mine < rows)
        table_ref[2 * nb + count] = i
        take = jnp.where(owned, mine, jnp.where(me == 0, partner, 0))
        send_ref[i // slots, pl.ds(i % slots, 1), :] = matrix_ref[pl.ds(take, 1), :]
        return count + jnp.where(owned & (row >= nb), 1, 0)

    count = lax.fori_loop(0, nb, place, 0, unroll=8)
    table_ref[3 * nb] = count
    lower_piece = panel_ref[:, :nb]
    for d in range(send_ref.shape[0]):
        send_ref[d, slots:, :] = lower_piece


def sort_kernel(table_ref, arrived_ref, panel_ref, send_ref, pieces_ref):
    planes = arrived_ref.shape[0]
    rows = panel_ref.shape[1]
    slots = send_ref.shape[1] // 2
    me = lax.axis_index("prow")
    for k in range(slots):
        owner = table_ref[me * slots + k] // rows
        send_ref[0, k : k + 1, :] = arrived_ref[owner, k : k + 1, :]
    send_ref[0, slots:, :] = arrived_ref[0, :slots, :]
    both = send_ref[0]
    for d in range(1, planes):
        send_ref[d] = both
    pieces_ref[:, :rows] = panel_ref[...]
    pieces_ref[:, rows:] = arrived_ref[0, slots:, :]


def invert_upper(block):
    size = block.shape[0]
    row = lax.broadcasted_iota(jnp.int32, (size, size), 0)
    col = lax.broadcasted_iota(jnp.int32, (size, size), 1)
    inverse = None
    width = 1
    while width < size:
        pair = ((row ^ col) & ~(2 * width - 1)) == 0
        cross = jnp.where(pair & ((row & width) == 0) & ((col & width) != 0), block, 0.0)
        if inverse is None:
            inverse = jnp.where(row == col, 1.0, 0.0) - cross
        else:
            inverse = inverse - dot(dot(inverse, cross), inverse)
        width *= 2
    return inverse


def update_kernel(table_ref, gathered_ref, arrived_ref, matrix_ref, out_ref, upper_ref):
    nb = upper_ref.shape[0]
    rows = matrix_ref.shape[0]
    planes = arrived_ref.shape[0]
    slots = nb // planes
    half = nb // 2
    me = lax.axis_index("prow")
    first = invert_upper(gathered_ref[:half, rows : rows + half])
    second = invert_upper(gathered_ref[half:, rows + half :])
    for d in range(planes):
        upper_ref[d * slots : (d + 1) * slots, :] = arrived_ref[d, :slots, :]
    top = dot_lhs_t(first, upper_ref[:half])
    rest = upper_ref[half:] - dot_lhs_t(gathered_ref[:half, rows + half :], top)
    upper_ref[:half] = top
    upper_ref[half:] = dot_lhs_t(second, rest)
    out_ref[...] = matrix_ref[...]

    def patch(n, _):
        slot = table_ref[2 * nb + n]
        target = table_ref[slot] - me * rows
        far = arrived_ref[slot // slots, pl.ds(slots + slot % slots, 1), :]
        near = matrix_ref[pl.ds(jnp.where(me == 0, table_ref[nb + slot], 0), 1), :]
        out_ref[pl.ds(target, 1), :] = jnp.where(me == 0, near, far)
        return 0

    lax.fori_loop(0, table_ref[3 * nb], patch, 0)
    out_ref[...] -= dot_lhs_t(gathered_ref[:, :rows], upper_ref[...])

    @pl.when(me == 0)
    def _():
        out_ref[:nb, :] = upper_ref[...]


def call(kernel, outs, in_specs, out_specs, scratch=()):
    return pl.pallas_call(
        kernel,
        out_shape=outs,
        in_specs=in_specs,
        out_specs=out_specs,
        scratch_shapes=list(scratch),
        compiler_params=pltpu.CompilerParams(vmem_limit_bytes=16 * 1024 * 1024),
    )


def local(matrix, factored_panel, pivots):
    rows, cols = matrix.shape
    nb = pivots.shape[0]
    planes = lax.axis_size("prow")
    slots = nb // planes
    width = factored_panel.shape[1]
    f32 = jnp.float32
    panel = factored_panel.T
    send, table = call(
        pack_kernel,
        (
            jax.ShapeDtypeStruct((planes, slots + width, cols), f32),
            jax.ShapeDtypeStruct((4 * nb,), jnp.int32),
        ),
        [SMEM, VMEM, VMEM],
        (VMEM, SMEM),
        [pltpu.SMEM((rows * planes,), jnp.int32)],
    )(pivots, matrix, panel)
    arrived = lax.all_to_all(send, "prow", 0, 0)
    send, pieces = call(
        sort_kernel,
        (
            jax.ShapeDtypeStruct((planes, 2 * slots, cols), f32),
            jax.ShapeDtypeStruct((width, rows + nb), f32),
        ),
        [SMEM, VMEM, VMEM],
        (VMEM, VMEM),
    )(table, arrived, panel)
    gathered = lax.all_gather(pieces, "pcol", axis=0, tiled=True)
    arrived = lax.all_to_all(send, "prow", 0, 0)
    return call(
        update_kernel,
        jax.ShapeDtypeStruct((rows, cols), f32),
        [SMEM, VMEM, VMEM, VMEM],
        VMEM,
        [pltpu.VMEM((nb, cols), f32)],
    )(table, gathered, arrived, matrix)


def solution(mesh):
    return jax.shard_map(
        local,
        mesh=mesh,
        in_specs=(P("prow", "pcol"), P("prow", "pcol"), P()),
        out_specs=P("prow", "pcol"),
        check_vma=False,
    )
```

time: 1450 us -> 92.4 us (0.06)
  the two profiles are of different devices: /device:TPU:1 before, /device:TPU:20 now
where the time goes in v1:
time: 92.4 us; the launch traced here: 92 us
  blocking collectives  62 us (67%)
  Pallas kernels  16 us (17%)
  starting transfers between devices  6 us (6%)
  waiting for transfers between devices  5.51 us (6%)
  local copies, waits for them, and re-layouts  2.45 us (3%)
    all_to_all x1, blocking collectives, local(): arrived = lax.all_to_all(send, 'prow', 0, 0)  38.8 us
    all_gather x1, blocking collectives, local(): gathered = lax.all_gather(pieces, 'pcol', axis=0, tiled=True)  23.2 us
    pallas_call x1, Pallas kernels, local(): call(update_kernel, jax.ShapeDtypeStruct((rows, cols), f32), [SMEM, VMEM,...  7.58 us
    pallas_call x1, Pallas kernels, local(): call(pack_kernel, (jax.ShapeDtypeStruct((planes, slots + width, cols), f3...  6.94 us
    all_to_all x1, starting transfers between devices, local(): arrived = lax.all_to_all(send, 'prow', 0, 0)  6 us
    all_to_all x1, waiting for transfers between devices, local(): arrived = lax.all_to_all(send, 'prow', 0, 0)  5.51 us
    unnamed x10, local copies, waits for them, and re-layouts  2.45 us
  transfers between devices with their start and end apart: 1, of which 1 were waited for; matrix products, arithmetic and copies ran while one was open for 0% of the time, Pallas kernels for 0%

profile of v1, /device:TPU:20, one launch (start us, length us, event | category | flops | bytes accessed | tf_op | source)
XLA Modules:
  0.0 92.0 jit_solution(7158090912079997549)
XLA Ops:
  0.0 0.0 copy-start.4
  0.0 0.7 copy-done.4
  0.7 0.0 copy-start
  0.7 1.0 %copy-done = f32[512,256]{1,0:T(8,128)S(1)} copy-done((f32[512,256]{1,0:T(8,128)S(1)}, f32[512,256]{1,0:T(8,128)}, u32[]{:S(2)}) %copy-start) | copy-done | bytes 524312
  1.7 0.0 copy-start.2
  1.7 0.7 copy-done.2
  2.4 6.9 %shard_map.37 = (f32[16,24,256]{2,1,0:T(8,128)S(1)}, s32[1024]{0:T(1024)S(1)}) custom-call(s32[256]{0:T(256)S(1)} %copy-done.4, f32[512,256]{1,0:T(8,128)S(1)} %copy-done, f32[8,512]{1,0:T(8,128)S(1)} %bitcast.1), custom_call_target="tpu_custom_call" | custom-call | tf_op jit(solution)/shard_map/pallas_call | solution.py:151
  9.4 0.0 copy-start.3
  9.4 38.8 %all_to_all.10.arrived_ref = f32[16,24,256]{2,1,0:T(8,128)S(1)} all-to-all(f32[16,24,256]{2,1,0:T(8,128)S(1)} %get-tuple-element.10), channel_id=1, replica_groups=mesh['prow'=16,'pcol'=32] {'prow'}, dimensions={0} | all-to-all | bytes 786432 | tf_op jit(solution)/shard_map/all_to_all | solution.py:161
  48.2 0.0 copy-done.3
  48.2 1.5 %shard_map.38 = (f32[16,32,256]{2,1,0:T(8,128)}, f32[8,768]{1,0:T(8,128)S(1)}) custom-call(s32[1024]{0:T(1024)S(1)} %get-tuple-element.9.table_ref, f32[16,24,256]{2,1,0:T(8,128)S(1)} %all_to_all.10.arrived_ref, f32[8,512]{1,0:T(8,128)S(1)} %bitcast.2), custom_call_target="tpu_custom_call" | custom-call | tf_op jit(solution)/shard_map/pallas_call | solution.py:162
  49.7 6.0 %all-to-all-start.1 = ((f32[16,32,256]{2,1,0:T(8,128)}), f32[16,32,256]{2,1,0:T(8,128)S(1)}, u32[]{:S(2)}, u32[]{:S(2)}) async-start(f32[16,32,256]{2,1,0:T(8,128)} %get-tuple-element.12), calls=%async_computation.1 | async-start | bytes 1048576 | tf_op jit(solution)/shard_map/all_to_all | solution.py:172
  55.7 0.0 copy-start.1
  55.7 23.2 %all_gather.3.gathered_ref = f32[256,768]{1,0:T(8,128)S(1)} all-gather(f32[8,768]{1,0:T(8,128)S(1)} %get-tuple-element.11), channel_id=1, replica_groups=mesh['prow'=16,'pcol'=32] {'pcol'}, dimensions={0}, use_global_device_ids=true | all-gather | bytes 811008 | tf_op jit(solution)/shard_map/all_gather | solution.py:171
  78.9 5.5 %all-to-all-done.1.arrived_ref = f32[16,32,256]{2,1,0:T(8,128)S(1)} async-done(((f32[16,32,256]{2,1,0:T(8,128)}), f32[16,32,256]{2,1,0:T(8,128)S(1)}, u32[]{:S(2)}, u32[]{:S(2)}) %all-to-all-start.1) | async-done | bytes 524320 | tf_op jit(solution)/shard_map/all_to_all | solution.py:172
  84.4 0.0 copy-done.1
  84.4 7.6 %shard_map.39 = f32[512,256]{1,0:T(8,128)} custom-call(s32[1024]{0:T(1024)S(1)} %get-tuple-element.9.table_ref, f32[256,768]{1,0:T(8,128)S(1)} %all_gather.3.gathered_ref, f32[16,32,256]{2,1,0:T(8,128)S(1)} %all-to-all-done.1.arrived_ref, f32[512,256]{1,0:T(8,128)S(1)} %copy-done.1), custom_call_target="tpu_custom_call" | custom-call | tf_op jit(solution)/shard_map/pallas_call | solution.py:173
Async XLA Ops:
  0.0 0.7 copy-start.4
  0.7 1.0 %copy-start = (f32[512,256]{1,0:T(8,128)S(1)}, f32[512,256]{1,0:T(8,128)}, u32[]{:S(2)}) copy-start(f32[512,256]{1,0:T(8,128)} %matrix_ref.3) | copy-start | bytes 1572868
  1.7 0.7 copy-start.2
  9.4 38.8 %copy-start.3 = (f32[512,8]{0,1:T(8,128)S(1)}, f32[512,8]{0,1:T(8,128)}, u32[]{:S(2)}) copy-start(f32[512,8]{0,1:T(8,128)} %param.4) | copy-start | bytes 49156
  49.7 34.7 %all-to-all-start.1 = ((f32[16,32,256]{2,1,0:T(8,128)}), f32[16,32,256]{2,1,0:T(8,128)S(1)}, u32[]{:S(2)}, u32[]{:S(2)}) async-start(f32[16,32,256]{2,1,0:T(8,128)} %get-tuple-element.12), calls=%async_computation.1 | async-start | bytes 1048576 | tf_op jit(solution)/shard_map/all_to_all | solution.py:172
  55.7 28.7 %copy-start.1 = (f32[512,256]{1,0:T(8,128)S(1)}, f32[512,256]{1,0:T(8,128)}, u32[]{:S(2)}) copy-start(f32[512,256]{1,0:T(8,128)} %matrix_ref.3) | copy-start | bytes 1572868

commit v2 on v1

--- a/solution.py
+++ b/solution.py
@@ -7,6 +7,7 @@
 
 HIGHEST = lax.Precision.HIGHEST
 VMEM = pl.BlockSpec(memory_space=pltpu.VMEM)
+HBM = pl.BlockSpec(memory_space=pltpu.HBM)
 SMEM = pl.BlockSpec(memory_space=pltpu.SMEM)
 
 
@@ -20,11 +21,16 @@
     return jnp.dot(a, b, precision=HIGHEST, preferred_element_type=jnp.float32)
 
 
-def pack_kernel(pivots_ref, matrix_ref, panel_ref, send_ref, table_ref, order_ref):
+def pack_kernel(pivots_ref, matrix_hbm, panel_hbm, send_ref, table_ref, order_ref, matrix_ref, panel_ref, sem):
     nb = pivots_ref.shape[0]
     rows = matrix_ref.shape[0]
-    slots = nb // send_ref.shape[0]
+    planes = send_ref.shape[0]
+    slots = nb // planes
     me = lax.axis_index("prow")
+    fetch_matrix = pltpu.make_async_copy(matrix_hbm, matrix_ref, sem.at[0])
+    fetch_panel = pltpu.make_async_copy(panel_hbm, panel_ref, sem.at[1])
+    fetch_matrix.start()
+    fetch_panel.start()
 
     def start(j, _):
         target = pivots_ref[j]
@@ -32,7 +38,7 @@
         order_ref[j] = j
         return 0
 
-    lax.fori_loop(0, nb, start, 0, unroll=8)
+    lax.fori_loop(0, nb, start, 0, unroll=16)
 
     def exchange(j, _):
         target = pivots_ref[j]
@@ -42,25 +48,31 @@
         order_ref[target] = first
         return 0
 
-    lax.fori_loop(0, nb, exchange, 0, unroll=8)
-
-    def place(i, count):
-        row = order_ref[i]
-        partner = order_ref[row]
-        table_ref[i] = row
-        table_ref[nb + i] = partner
-        mine = row - me * rows
-        owned = (mine >= 0) & (mine < rows)
-        table_ref[2 * nb + count] = i
-        take = jnp.where(owned, mine, jnp.where(me == 0, partner, 0))
-        send_ref[i // slots, pl.ds(i % slots, 1), :] = matrix_ref[pl.ds(take, 1), :]
-        return count + jnp.where(owned & (row >= nb), 1, 0)
-
-    count = lax.fori_loop(0, nb, place, 0, unroll=8)
-    table_ref[3 * nb] = count
+    lax.fori_loop(0, nb, exchange, 0, unroll=16)
+    fetch_panel.wait()
     lower_piece = panel_ref[:, :nb]
-    for d in range(send_ref.shape[0]):
+    for d in range(planes):
         send_ref[d, slots:, :] = lower_piece
+    fetch_matrix.wait()
+    base = me * rows
+
+    def place(d, count):
+        for k in range(slots):
+            i = d * slots + k
+            row = order_ref[i]
+            partner = order_ref[row]
+            mine = row - base
+            owned = (mine >= 0) & (mine < rows)
+            table_ref[i] = row
+            table_ref[nb + count] = i
+            table_ref[2 * nb + count] = mine
+            table_ref[3 * nb + count] = partner
+            take = jnp.where(owned, mine, jnp.where(me == 0, partner, 0))
+            send_ref[d, k : k + 1, :] = matrix_ref[pl.ds(take, 1), :]
+            count = count + jnp.where(owned & (row >= nb), 1, 0)
+        return count
+
+    table_ref[4 * nb] = lax.fori_loop(0, planes, place, 0)
 
 
 def sort_kernel(table_ref, arrived_ref, panel_ref, send_ref, pieces_ref):
@@ -68,6 +80,8 @@
     rows = panel_ref.shape[1]
     slots = send_ref.shape[1] // 2
     me = lax.axis_index("prow")
+    pieces_ref[:, :rows] = panel_ref[...]
+    pieces_ref[:, rows:] = arrived_ref[0, slots:, :]
     for k in range(slots):
         owner = table_ref[me * slots + k] // rows
         send_ref[0, k : k + 1, :] = arrived_ref[owner, k : k + 1, :]
@@ -75,8 +89,6 @@
     both = send_ref[0]
     for d in range(1, planes):
         send_ref[d] = both
-    pieces_ref[:, :rows] = panel_ref[...]
-    pieces_ref[:, rows:] = arrived_ref[0, slots:, :]
 
 
 def invert_upper(block):
@@ -96,32 +108,36 @@
     return inverse
 
 
-def update_kernel(table_ref, gathered_ref, arrived_ref, matrix_ref, out_ref, upper_ref):
+def invert_kernel(gathered_ref, inverse_ref):
+    half = inverse_ref.shape[0] // 2
+    rows = gathered_ref.shape[1] - 2 * half
+    inverse_ref[:half] = invert_upper(gathered_ref[:half, rows : rows + half])
+    inverse_ref[half:] = invert_upper(gathered_ref[half:, rows + half :])
+
+
+def update_kernel(table_ref, gathered_ref, inverse_ref, arrived_ref, matrix_ref, out_ref, upper_ref):
     nb = upper_ref.shape[0]
     rows = matrix_ref.shape[0]
     planes = arrived_ref.shape[0]
     slots = nb // planes
     half = nb // 2
     me = lax.axis_index("prow")
-    first = invert_upper(gathered_ref[:half, rows : rows + half])
-    second = invert_upper(gathered_ref[half:, rows + half :])
     for d in range(planes):
         upper_ref[d * slots : (d + 1) * slots, :] = arrived_ref[d, :slots, :]
-    top = dot_lhs_t(first, upper_ref[:half])
+    top = dot_lhs_t(inverse_ref[:half], upper_ref[:half])
     rest = upper_ref[half:] - dot_lhs_t(gathered_ref[:half, rows + half :], top)
     upper_ref[:half] = top
-    upper_ref[half:] = dot_lhs_t(second, rest)
+    upper_ref[half:] = dot_lhs_t(inverse_ref[half:], rest)
     out_ref[...] = matrix_ref[...]
 
     def patch(n, _):
-        slot = table_ref[2 * nb + n]
-        target = table_ref[slot] - me * rows
+        slot = table_ref[nb + n]
         far = arrived_ref[slot // slots, pl.ds(slots + slot % slots, 1), :]
-        near = matrix_ref[pl.ds(jnp.where(me == 0, table_ref[nb + slot], 0), 1), :]
-        out_ref[pl.ds(target, 1), :] = jnp.where(me == 0, near, far)
+        near = matrix_ref[pl.ds(jnp.where(me == 0, table_ref[3 * nb + n], 0), 1), :]
+        out_ref[pl.ds(table_ref[2 * nb + n], 1), :] = jnp.where(me == 0, near, far)
         return 0
 
-    lax.fori_loop(0, table_ref[3 * nb], patch, 0)
+    lax.fori_loop(0, table_ref[4 * nb], patch, 0)
     out_ref[...] -= dot_lhs_t(gathered_ref[:, :rows], upper_ref[...])
 
     @pl.when(me == 0)
@@ -152,11 +168,16 @@
         pack_kernel,
         (
             jax.ShapeDtypeStruct((planes, slots + width, cols), f32),
-            jax.ShapeDtypeStruct((4 * nb,), jnp.int32),
+            jax.ShapeDtypeStruct((8 * nb,), jnp.int32),
         ),
-        [SMEM, VMEM, VMEM],
+        [SMEM, HBM, HBM],
         (VMEM, SMEM),
-        [pltpu.SMEM((rows * planes,), jnp.int32)],
+        [
+            pltpu.SMEM((rows * planes,), jnp.int32),
+            pltpu.VMEM((rows, cols), f32),
+            pltpu.VMEM((width, rows), f32),
+            pltpu.SemaphoreType.DMA((2,)),
+        ],
     )(pivots, matrix, panel)
     arrived = lax.all_to_all(send, "prow", 0, 0)
     send, pieces = call(
@@ -170,13 +191,14 @@
     )(table, arrived, panel)
     gathered = lax.all_gather(pieces, "pcol", axis=0, tiled=True)
     arrived = lax.all_to_all(send, "prow", 0, 0)
+    inverse = call(invert_kernel, jax.ShapeDtypeStruct((nb, nb // 2), f32), [VMEM], VMEM)(gathered)
     return call(
         update_kernel,
         jax.ShapeDtypeStruct((rows, cols), f32),
-        [SMEM, VMEM, VMEM, VMEM],
+        [SMEM, VMEM, VMEM, VMEM, VMEM],
         VMEM,
         [pltpu.VMEM((nb, cols), f32)],
-    )(table, gathered, arrived, matrix)
+    )(table, gathered, inverse, arrived, matrix)
 
 
 def solution(mesh):

time: 92.4 us -> 89 us (0.963)
  the two profiles are of different devices: /device:TPU:20 before, /device:TPU:1 now
where the time goes in v2:
time: 89 us; the launch traced here: 88.6 us
  blocking collectives  59.8 us (67%)
  Pallas kernels  14.8 us (17%)
  starting transfers between devices  11.5 us (13%)
  local copies, waits for them, and re-layouts  2.45 us (3%)
    all_to_all x1, blocking collectives, local(): arrived = lax.all_to_all(send, 'prow', 0, 0)  33.5 us
    all_gather x1, blocking collectives, local(): gathered = lax.all_gather(pieces, 'pcol', axis=0, tiled=True)  26.2 us
    all_to_all x1, starting transfers between devices, local(): arrived = lax.all_to_all(send, 'prow', 0, 0)  11.5 us
    pallas_call x1, Pallas kernels, local(): call(pack_kernel, (jax.ShapeDtypeStruct((planes, slots + width, cols), f3...  5.11 us
    pallas_call x1, Pallas kernels, local(): call(invert_kernel, jax.ShapeDtypeStruct((nb, nb // 2), f32), [VMEM], VMEM)  4.68 us
    pallas_call x1, Pallas kernels, local(): call(update_kernel, jax.ShapeDtypeStruct((rows, cols), f32), [SMEM, VMEM,...  3.46 us
    unnamed x10, local copies, waits for them, and re-layouts  2.45 us
  transfers between devices with their start and end apart: 1, of which 0 were waited for; matrix products, arithmetic and copies ran while one was open for 0% of the time, Pallas kernels for 5%

profile of v2, /device:TPU:1, one launch (start us, length us, event | category | flops | bytes accessed | tf_op | source)
XLA Modules:
  0.0 88.6 jit_solution(2207481891819579697)
XLA Ops:
  0.0 0.0 copy-start.4
  0.0 0.7 copy-done.4
  0.7 0.0 copy-start
  0.7 1.0 %copy-done = f32[512,256]{1,0:T(8,128)S(1)} copy-done((f32[512,256]{1,0:T(8,128)S(1)}, f32[512,256]{1,0:T(8,128)}, u32[]{:S(2)}) %copy-start) | copy-done | bytes 524312
  1.7 0.0 copy-start.2
  1.7 0.7 copy-done.2
  2.4 5.1 %shard_map.37 = (f32[16,24,256]{2,1,0:T(8,128)S(1)}, s32[2048]{0:T(1024)S(1)}) custom-call(s32[256]{0:T(256)S(1)} %copy-done.4, f32[512,256]{1,0:T(8,128)S(1)} %copy-done, f32[8,512]{1,0:T(8,128)S(1)} %bitcast.1), custom_call_target="tpu_custom_call" | custom-call | tf_op jit(solution)/shard_map/pallas_call | solution.py:167
  7.6 0.0 copy-start.3
  7.6 33.5 %all_to_all.10.arrived_ref = f32[16,24,256]{2,1,0:T(8,128)S(1)} all-to-all(f32[16,24,256]{2,1,0:T(8,128)S(1)} %get-tuple-element.10), channel_id=1, replica_groups=mesh['prow'=16,'pcol'=32] {'prow'}, dimensions={0} | all-to-all | bytes 786432 | tf_op jit(solution)/shard_map/all_to_all | solution.py:182
  41.1 0.0 copy-done.3
  41.1 1.6 %shard_map.38 = (f32[16,32,256]{2,1,0:T(8,128)}, f32[8,768]{1,0:T(8,128)S(1)}) custom-call(s32[2048]{0:T(1024)S(1)} %get-tuple-element.9.table_ref, f32[16,24,256]{2,1,0:T(8,128)S(1)} %all_to_all.10.arrived_ref, f32[8,512]{1,0:T(8,128)S(1)} %bitcast.2), custom_call_target="tpu_custom_call" | custom-call | tf_op jit(solution)/shard_map/pallas_call | solution.py:183
  42.7 11.5 %all-to-all-start.1 = ((f32[16,32,256]{2,1,0:T(8,128)}), f32[16,32,256]{2,1,0:T(8,128)S(1)}, u32[]{:S(2)}, u32[]{:S(2)}) async-start(f32[16,32,256]{2,1,0:T(8,128)} %get-tuple-element.12), calls=%async_computation.1 | async-start | bytes 1048576 | tf_op jit(solution)/shard_map/all_to_all | solution.py:193
  54.2 26.2 %all_gather.3.gathered_ref = f32[256,768]{1,0:T(8,128)S(1)} all-gather(f32[8,768]{1,0:T(8,128)S(1)} %get-tuple-element.11), channel_id=1, replica_groups=mesh['prow'=16,'pcol'=32] {'pcol'}, dimensions={0}, use_global_device_ids=true | all-gather | bytes 811008 | tf_op jit(solution)/shard_map/all_gather | solution.py:192
  80.4 0.0 copy-start.1
  80.4 4.7 %shard_map.39.inverse_ref = f32[256,128]{1,0:T(8,128)S(1)} custom-call(f32[256,768]{1,0:T(8,128)S(1)} %all_gather.3.gathered_ref), custom_call_target="tpu_custom_call" | custom-call | tf_op jit(solution)/shard_map/pallas_call | solution.py:194
  85.1 0.0 all-to-all-done.1.arrived_ref
  85.1 0.0 copy-done.1
  85.1 3.5 %shard_map.40 = f32[512,256]{1,0:T(8,128)} custom-call(s32[2048]{0:T(1024)S(1)} %get-tuple-element.9.table_ref, f32[256,768]{1,0:T(8,128)S(1)} %all_gather.3.gathered_ref, f32[256,128]{1,0:T(8,128)S(1)} %shard_map.39.inverse_ref, f32[16,32,256]{2,1,0:T(8,128)S(1)} %all-to-all-done.1.arrived_ref, f32[512,256]{1,0:T(8,128)S(1)} %copy-done.1), custom_call_target="tpu_custom_call" | custom-call | tf_op jit(solution)/shard_map/pallas_call | solution.py:195
Async XLA Ops:
  0.0 0.7 copy-start.4
  0.7 1.0 %copy-start = (f32[512,256]{1,0:T(8,128)S(1)}, f32[512,256]{1,0:T(8,128)}, u32[]{:S(2)}) copy-start(f32[512,256]{1,0:T(8,128)} %matrix_ref.1) | copy-start | bytes 1572868
  1.7 0.7 copy-start.2
  7.6 33.6 %copy-start.3 = (f32[512,8]{0,1:T(8,128)S(1)}, f32[512,8]{0,1:T(8,128)}, u32[]{:S(2)}) copy-start(f32[512,8]{0,1:T(8,128)} %param.4) | copy-start | bytes 49156
  42.7 42.4 %all-to-all-start.1 = ((f32[16,32,256]{2,1,0:T(8,128)}), f32[16,32,256]{2,1,0:T(8,128)S(1)}, u32[]{:S(2)}, u32[]{:S(2)}) async-start(f32[16,32,256]{2,1,0:T(8,128)} %get-tuple-element.12), calls=%async_computation.1 | async-start | bytes 1048576 | tf_op jit(solution)/shard_map/all_to_all | solution.py:193
  80.4 4.7 %copy-start.1 = (f32[512,256]{1,0:T(8,128)S(1)}, f32[512,256]{1,0:T(8,128)}, u32[]{:S(2)}) copy-start(f32[512,256]{1,0:T(8,128)} %matrix_ref.1) | copy-start | bytes 1572868

commit v3 on v2

v3 whole, which is shorter than its diff:
```python
from functools import partial

import jax
import jax.numpy as jnp
from jax import lax
from jax.experimental import pallas as pl
from jax.experimental.pallas import tpu as pltpu
from jax.sharding import PartitionSpec as P

HIGHEST = lax.Precision.HIGHEST
ROUND = 48
EARLY = 4
MAIN = 0
VMEM = pl.BlockSpec(memory_space=pltpu.VMEM)
HBM = pl.BlockSpec(memory_space=pltpu.HBM)
SMEM = pl.BlockSpec(memory_space=pltpu.SMEM)


def dot(a, b):
    return jnp.dot(a, b, precision=HIGHEST, preferred_element_type=jnp.float32)


class Table:
    ROW, PARTNER, PLACE, OWN, COUNT = range(5)


def spread_kernel(panel_ref, send_ref):
    nb = send_ref.shape[2]
    piece = panel_ref[:, :nb]
    for d in range(send_ref.shape[0]):
        send_ref[d] = piece


def join_kernel(panel_ref, pieces_ref, out_ref):
    rows = panel_ref.shape[1]
    out_ref[:, :rows] = panel_ref[...]
    out_ref[:, rows:] = pieces_ref[EARLY % pieces_ref.shape[0]]


def pack_kernel(pivots_ref, matrix_hbm, send_ref, table_ref, order_ref, count_ref, matrix_ref, sem):
    nb = pivots_ref.shape[0]
    rows = matrix_ref.shape[0]
    planes = count_ref.shape[0]
    room = send_ref.shape[0] // planes
    me = lax.axis_index("prow")
    bits = rows.bit_length() - 1
    fetch_matrix = pltpu.make_async_copy(matrix_hbm, matrix_ref, sem)
    fetch_matrix.start()

    def start(j, _):
        target = pivots_ref[j]
        order_ref[target] = target
        order_ref[j] = j
        return 0

    lax.fori_loop(0, nb, start, 0, unroll=16)

    def exchange(j, _):
        target = pivots_ref[j]
        first = order_ref[j]
        second = order_ref[target]
        order_ref[j] = second
        order_ref[target] = first
        return 0

    lax.fori_loop(0, nb, exchange, 0, unroll=16)
    for d in range(planes):
        count_ref[d] = 0

    def tally(i, _):
        row = order_ref[i]
        partner = order_ref[row]
        owner = row >> bits
        nth = count_ref[owner]
        count_ref[owner] = nth + 1
        table_ref[Table.ROW * nb + i] = row
        table_ref[Table.PARTNER * nb + i] = partner
        table_ref[Table.PLACE * nb + i] = ((owner + MAIN) & (planes - 1)) * room + jnp.minimum(nth, room - 1)
        table_ref[jnp.where(owner == me, Table.OWN * nb + nth, Table.COUNT * nb)] = i
        return 0

    lax.fori_loop(0, nb, tally, 0, unroll=16)
    table_ref[Table.COUNT * nb] = count_ref[me]
    most = count_ref[1]
    for d in range(2, planes):
        most = jnp.maximum(most, count_ref[d])
    table_ref[Table.COUNT * nb + 1] = jnp.where(count_ref[0] + most <= room, 1, 0)
    fetch_matrix.wait()

    def give(n, _):
        send_ref[pl.ds(n, 1), :] = matrix_ref[pl.ds(table_ref[Table.ROW * nb + table_ref[Table.OWN * nb + n]] & (rows - 1), 1), :]
        return 0

    lax.fori_loop(0, jnp.minimum(count_ref[me], room), give, 0)
    given = send_ref[:room, :]
    for d in range(1, planes):
        send_ref[d * room : (d + 1) * room, :] = given

    @pl.when(me == 0)
    def _():
        def hand(i, _):
            place = table_ref[Table.PLACE * nb + i]
            owner = table_ref[Table.ROW * nb + i] >> bits
            away = owner > 0
            partner = jnp.where(away, table_ref[Table.PARTNER * nb + i], 0)
            put = 2 * ((owner + MAIN) & (planes - 1)) * room + room - 1 - place
            put = jnp.where(away, put, MAIN * room + room - 1)
            send_ref[pl.ds(put, 1), :] = matrix_ref[pl.ds(partner, 1), :]
            return 0

        lax.fori_loop(0, nb, hand, 0, unroll=16)


def slot_kernel(table_ref, matrix_ref, send_ref):
    planes, slots, _ = send_ref.shape
    nb = planes * slots
    rows = matrix_ref.shape[0]
    me = lax.axis_index("prow")

    def place(d, _):
        for k in range(slots):
            i = d * slots + k
            mine = table_ref[Table.ROW * nb + i] - me * rows
            owned = (mine >= 0) & (mine < rows)
            take = jnp.where(owned, mine, jnp.where(me == 0, table_ref[Table.PARTNER * nb + i], 0))
            send_ref[d, k : k + 1, :] = matrix_ref[pl.ds(take, 1), :]
        return 0

    lax.fori_loop(0, planes, place, 0)


def sort_kernel(rows, table_ref, arrived_ref, send_ref):
    planes, slots, _ = arrived_ref.shape
    me = lax.axis_index("prow")
    for k in range(slots):
        owner = table_ref[me * slots + k] // rows
        send_ref[0, k : k + 1, :] = arrived_ref[owner, k : k + 1, :]
    send_ref[0, slots:, :] = arrived_ref[0]
    both = send_ref[0]
    for d in range(1, planes):
        send_ref[d] = both


def invert_upper(block):
    size = block.shape[0]
    row = lax.broadcasted_iota(jnp.int32, (size, size), 0)
    col = lax.broadcasted_iota(jnp.int32, (size, size), 1)
    inverse = None
    width = 1
    while width < size:
        pair = ((row ^ col) & ~(2 * width - 1)) == 0
        cross = jnp.where(pair & ((row & width) == 0) & ((col & width) != 0), block, 0.0)
        if inverse is None:
            inverse = jnp.where(row == col, 1.0, 0.0) - cross
        else:
            inverse = inverse - dot(dot(inverse, cross), inverse)
        width *= 2
    return inverse


def invert_kernel(gathered_ref, panel_ref, inverse_ref, lower_ref):
    rows, nb = panel_ref.shape
    half = nb // 2
    inverse_ref[:half] = invert_upper(gathered_ref[:half, rows : rows + half]).T
    inverse_ref[half:] = invert_upper(gathered_ref[half:, rows + half :]).T
    lower_ref[...] = gathered_ref[:half, rows + half :].T
    panel_ref[...] = gathered_ref[:, :rows].T


def update_kernel(one_round, table_ref, panel_ref, inverse_ref, lower_ref, arrived_ref, matrix_ref, out_ref, upper_ref):
    planes, slots, cols = upper_ref.shape
    nb = planes * slots
    rows = matrix_ref.shape[0]
    room = arrived_ref.shape[0] // planes
    half = nb // 2
    me = lax.axis_index("prow")

    def pick(d, _):
        for k in range(slots):
            place = table_ref[Table.PLACE * nb + d * slots + k] if one_round else d * room + k
            upper_ref[d, k : k + 1, :] = arrived_ref[pl.ds(place, 1), :]
        return 0

    lax.fori_loop(0, planes, pick, 0)
    out_ref[...] = matrix_ref[...]

    def patch(n, _):
        slot = table_ref[Table.OWN * nb + n]
        if one_round:
            place = MAIN * room + jnp.where(me == 0, 0, room - 1 - n)
        else:
            place = slot // slots * room + slots + slot % slots
        far = arrived_ref[pl.ds(place, 1), :]
        lands = jnp.where(me == 0, jnp.minimum(table_ref[Table.PARTNER * nb + slot], rows - 1), 0)
        near = matrix_ref[pl.ds(lands, 1), :]
        out_ref[pl.ds(table_ref[Table.ROW * nb + slot] - me * rows, 1), :] = jnp.where(me == 0, near, far)
        return 0

    lax.fori_loop(0, table_ref[Table.COUNT * nb], patch, 0)
    upper = upper_ref[...].reshape(nb, cols)
    top = dot(inverse_ref[:half], upper[:half])
    rest = upper[half:] - dot(lower_ref[...], top)
    upper = jnp.concatenate([top, dot(inverse_ref[half:], rest)], axis=0)
    out_ref[...] -= dot(panel_ref[...], upper)

    @pl.when(me == 0)
    def _():
        out_ref[:nb, :] = upper


def call(kernel, outs, in_specs, out_specs, scratch=()):
    return pl.pallas_call(
        kernel,
        out_shape=outs,
        in_specs=in_specs,
        out_specs=out_specs,
        scratch_shapes=list(scratch),
        compiler_params=pltpu.CompilerParams(vmem_limit_bytes=16 * 1024 * 1024),
    )


def exchange(value, place):
    planes = value.shape[0]
    order = [[(p - place) % planes for p in range(planes)]]
    return lax.all_to_all(value, "prow", 0, 0, axis_index_groups=order)


def local(matrix, factored_panel, pivots):
    rows, cols = matrix.shape
    nb = pivots.shape[0]
    planes = lax.axis_size("prow")
    slots = nb // planes
    width = factored_panel.shape[1]
    room = min(ROUND, nb)
    f32 = jnp.float32
    panel = factored_panel.T
    pieces = call(spread_kernel, jax.ShapeDtypeStruct((planes, width, nb), f32), [VMEM], VMEM)(panel)
    pieces = exchange(pieces, EARLY)
    send, table = call(
        pack_kernel,
        (
            jax.ShapeDtypeStruct((planes * room, cols), f32),
            jax.ShapeDtypeStruct((8 * nb,), jnp.int32),
        ),
        [SMEM, HBM],
        (VMEM, SMEM),
        [
            pltpu.SMEM((rows * planes,), jnp.int32),
            pltpu.SMEM((planes,), jnp.int32),
            pltpu.VMEM((rows, cols), f32),
            pltpu.SemaphoreType.DMA,
        ],
    )(pivots, matrix)

    def finish(one_round, table, panel, pieces, arrived, matrix):
        pieces = call(join_kernel, jax.ShapeDtypeStruct((width, rows + nb), f32), [VMEM, VMEM], VMEM)(panel, pieces)
        gathered = lax.all_gather(pieces, "pcol", axis=0, tiled=True)
        by_rows = call(
            invert_kernel,
            (
                jax.ShapeDtypeStruct((rows, nb), f32),
                jax.ShapeDtypeStruct((nb, nb // 2), f32),
                jax.ShapeDtypeStruct((nb // 2, nb // 2), f32),
            ),
            [VMEM],
            (VMEM, VMEM, VMEM),
        )(gathered)
        return call(
            partial(update_kernel, one_round),
            jax.ShapeDtypeStruct((rows, cols), f32),
            [SMEM, VMEM, VMEM, VMEM, VMEM, VMEM],
            VMEM,
            [pltpu.VMEM((planes, slots, cols), f32)],
        )(table, *by_rows, arrived, matrix)

    def one_round(send, table, panel, pieces, matrix):
        arrived = exchange(send.reshape(planes, room, cols), MAIN)
        return finish(True, table, panel, pieces, arrived.reshape(planes * room, cols), matrix)

    def two_rounds(send, table, panel, pieces, matrix):
        slot = jax.ShapeDtypeStruct((planes, slots, cols), f32)
        both = jax.ShapeDtypeStruct((planes, 2 * slots, cols), f32)
        arrived = exchange(call(slot_kernel, slot, [SMEM, VMEM], VMEM)(table, matrix), 0)
        send = call(partial(sort_kernel, rows), both, [SMEM, VMEM], VMEM)(table, arrived)
        arrived = exchange(send, 0)
        return finish(False, table, panel, pieces, arrived.reshape(2 * nb, cols), matrix)

    fits = table[Table.COUNT * nb + 1] == 1
    return lax.cond(fits, one_round, two_rounds, send, table, panel, pieces, matrix)


def solution(mesh):
    return jax.shard_map(
        local,
        mesh=mesh,
        in_specs=(P("prow", "pcol"), P("prow", "pcol"), P()),
        out_specs=P("prow", "pcol"),
        check_vma=False,
    )
```

time: 89 us -> 76.7 us (0.86)
  the two profiles are of different devices: /device:TPU:1 before, /device:TPU:58 now
where the time goes in v3:
time: 76.7 us; the launch traced here: 76.3 us
  starting transfers between devices  23.6 us (31%)
  blocking collectives  23.3 us (30%)
  Pallas kernels  14.5 us (19%)
  waiting for transfers between devices  12.7 us (17%)
  local copies, waits for them, and re-layouts  1.46 us (2%)
    all_to_all x2, starting transfers between devices, exchange(): return lax.all_to_all(value, 'prow', 0, 0, axis_index_groups=order)  23.6 us
    all_gather x1, blocking collectives, finish(): gathered = lax.all_gather(pieces, 'pcol', axis=0, tiled=True)  23.3 us
    all_to_all x2, waiting for transfers between devices, exchange(): return lax.all_to_all(value, 'prow', 0, 0, axis_index_groups=order)  12.7 us
    pallas_call x1, Pallas kernels, local(): call(pack_kernel, (jax.ShapeDtypeStruct((planes * room, cols), f32), jax....  5.2 us
    pallas_call x1, Pallas kernels, finish(): call(invert_kernel, (jax.ShapeDtypeStruct((rows, nb), f32), jax.ShapeDtyp...  4.78 us
    pallas_call x1, Pallas kernels, finish(): call(partial(update_kernel, one_round), jax.ShapeDtypeStruct((rows, cols)...  3.16 us
  transfers between devices with their start and end apart: 2, of which 2 were waited for; matrix products, arithmetic and copies ran while one was open for 1% of the time, Pallas kernels for 13%

profile of v3, /device:TPU:58, one launch (start us, length us, event | category | flops | bytes accessed | tf_op | source)
XLA Modules:
  0.0 76.3 jit_solution(6674983352222326861)
XLA Ops:
  0.0 1.4 %shard_map.40 = f32[16,8,256]{2,1,0:T(8,128)} custom-call(f32[8,512]{1,0:T(8,128)} %bitcast.7), custom_call_target="tpu_custom_call" | custom-call | tf_op jit(solution)/shard_map/pallas_call | solution.py:237
  1.4 0.0 copy-start
  1.4 0.0 copy-start.1
  1.4 15.3 %all-to-all-start.3 = ((f32[16,8,256]{2,1,0:T(8,128)}), f32[16,8,256]{2,1,0:T(8,128)S(1)}, u32[]{:S(2)}, u32[]{:S(2)}) async-start(f32[16,8,256]{2,1,0:T(8,128)} %shard_map.40), calls=%async_computation.3 | async-start | bytes 262144 | tf_op jit(solution)/shard_map/all_to_all | solution.py:225
  16.7 0.0 copy-done
  16.7 0.0 copy-start.3
  16.7 5.2 %shard_map.39 = (f32[768,256]{1,0:T(8,128)}, s32[2048]{0:T(1024)S(1)}) custom-call(s32[256]{0:T(256)S(1)} %copy-done, f32[512,256]{1,0:T(8,128)} %matrix_hbm.1), custom_call_target="tpu_custom_call" | custom-call | tf_op jit(solution)/shard_map/pallas_call | solution.py:239
  22.0 0.7 slice.3
  23.3 3.6 %all-to-all-done.3 = f32[16,8,256]{2,1,0:T(8,128)S(1)} async-done(((f32[16,8,256]{2,1,0:T(8,128)}), f32[16,8,256]{2,1,0:T(8,128)S(1)}, u32[]{:S(2)}, u32[]{:S(2)}) %all-to-all-start.3) | async-done | bytes 131104 | tf_op jit(solution)/shard_map/all_to_all | solution.py:225
  26.9 0.0 copy-done.1
  26.9 0.0 copy-done.3
  26.9 48.6 %conditional.1 = (f32[512,256]{1,0:T(8,128)S(1)}) conditional(s32[]{:T(128)} %bitcast.3, (f32[8,512]{1,0:T(8,128)S(1)}, f32[16,8,256]{2,1,0:T(8,128)S(1)}, s32[2048]{0:T(1024)S(1)}, f32[512,256]{1,0:T(8,128)S(1)}) %tuple.20, (f32[8,512]{1,0:T(8,128)S(1)}, f32[16,8,256]{2,1,0:T(8,128)S(1)}, f32[768,256]{1,0:T(8,128)}, s32[2048]{0:T(1024)S(1)}, ...), branch_computations={%region_0.0_spmd, %region_1.0_spmd} | conditional | bytes 3170344 | solution.py:289
  26.9 8.3 %all-to-all-start.2 = ((f32[16,48,256]{2,1,0:T(8,128)}), f32[16,48,256]{2,1,0:T(8,128)S(1)}, u32[]{:S(2)}, u32[]{:S(2)}) async-start(f32[16,48,256]{2,1,0:T(8,128)} %bitcast.1), calls=%async_computation.2 | async-start | bytes 1572864 | tf_op jit(solution)/shard_map/cond/branch_1_fun/all_to_all | solution.py:225
  35.2 23.3 %all_gather.5.gathered_ref = f32[256,768]{1,0:T(8,128)S(1)} all-gather(f32[8,768]{1,0:T(8,128)S(1)} %branch_1_fun.3), channel_id=1, replica_groups=mesh['prow'=16,'pcol'=32] {'pcol'}, dimensions={0}, use_global_device_ids=true | all-gather | bytes 811008 | tf_op jit(solution)/shard_map/cond/branch_1_fun/all_gather | solution.py:257
  58.5 4.8 %branch_1_fun.4 = (f32[512,256]{1,0:T(8,128)S(1)}, f32[256,128]{1,0:T(8,128)S(1)}, f32[128,128]{1,0:T(8,128)S(1)}) custom-call(f32[256,768]{1,0:T(8,128)S(1)} %all_gather.5.gathered_ref), custom_call_target="tpu_custom_call" | custom-call | tf_op jit(solution)/shard_map/cond/branch_1_fun/pallas_call | solution.py:258
  63.3 9.1 %all-to-all-done.2 = f32[16,48,256]{2,1,0:T(8,128)S(1)} async-done(((f32[16,48,256]{2,1,0:T(8,128)}), f32[16,48,256]{2,1,0:T(8,128)S(1)}, u32[]{:S(2)}, u32[]{:S(2)}) %all-to-all-start.2) | async-done | bytes 786464 | tf_op jit(solution)/shard_map/cond/branch_1_fun/all_to_all | solution.py:225
  72.4 3.2 %branch_1_fun.5 = f32[512,256]{1,0:T(8,128)S(1)} custom-call(s32[2048]{0:T(1024)S(1)} %get-tuple-element.33.table_ref, f32[512,256]{1,0:T(8,128)S(1)} %get-tuple-element.36.panel_ref, f32[256,128]{1,0:T(8,128)S(1)} %get-tuple-element.37.inverse_ref, f32[128,128]{1,0:T(8,128)S(1)} %get-tuple-element.38.lower_ref, f32[768,256]{1,0:T(8,128)S(1)} %bitcast.5, ...), custom_call_target="tpu_custom_call" | custom-call | tf_op jit(solution)/shard_map/cond/branch_1_fun/pallas_call | solution.py:268
  75.5 0.0 copy-start.2
  75.6 0.8 %copy-done.2 = f32[512,256]{1,0:T(8,128)} copy-done((f32[512,256]{1,0:T(8,128)}, f32[512,256]{1,0:T(8,128)S(1)}, u32[]{:S(2)}) %copy-start.2) | copy-done | bytes 524312
  (1 shorter events, 0.0 us)
Async XLA Ops:
  1.4 15.4 %copy-start = (s32[256]{0:T(256)S(1)}, s32[256]{0:T(256)}, u32[]{:S(2)}) copy-start(s32[256]{0:T(256)} %pivots_ref.1) | copy-start | bytes 3076
  1.4 25.5 %copy-start.1 = (f32[512,256]{1,0:T(8,128)S(1)}, f32[512,256]{1,0:T(8,128)}, u32[]{:S(2)}) copy-start(f32[512,256]{1,0:T(8,128)} %matrix_hbm.1) | copy-start | bytes 1572868
  1.4 25.5 %all-to-all-start.3 = ((f32[16,8,256]{2,1,0:T(8,128)}), f32[16,8,256]{2,1,0:T(8,128)S(1)}, u32[]{:S(2)}, u32[]{:S(2)}) async-start(f32[16,8,256]{2,1,0:T(8,128)} %shard_map.40), calls=%async_computation.3 | async-start | bytes 262144 | tf_op jit(solution)/shard_map/all_to_all | solution.py:225
  16.7 10.2 %copy-start.3 = (f32[512,8]{0,1:T(8,128)S(1)}, f32[512,8]{0,1:T(8,128)}, u32[]{:S(2)}) copy-start(f32[512,8]{0,1:T(8,128)} %param.6) | copy-start | bytes 49156
  26.9 45.5 %all-to-all-start.2 = ((f32[16,48,256]{2,1,0:T(8,128)}), f32[16,48,256]{2,1,0:T(8,128)S(1)}, u32[]{:S(2)}, u32[]{:S(2)}) async-start(f32[16,48,256]{2,1,0:T(8,128)} %bitcast.1), calls=%async_computation.2 | async-start | bytes 1572864 | tf_op jit(solution)/shard_map/cond/branch_1_fun/all_to_all | solution.py:225
  75.5 0.8 %copy-start.2 = (f32[512,256]{1,0:T(8,128)}, f32[512,256]{1,0:T(8,128)S(1)}, u32[]{:S(2)}) copy-start(f32[512,256]{1,0:T(8,128)S(1)} %get-tuple-element.51) | copy-start | bytes 1572868

commit v4 on v3

--- a/solution.py
+++ b/solution.py
@@ -8,9 +8,9 @@
 from jax.sharding import PartitionSpec as P
 
 HIGHEST = lax.Precision.HIGHEST
-ROUND = 48
+ROUNDS = (40, 48)
 EARLY = 4
-MAIN = 0
+MAIN = 4
 VMEM = pl.BlockSpec(memory_space=pltpu.VMEM)
 HBM = pl.BlockSpec(memory_space=pltpu.HBM)
 SMEM = pl.BlockSpec(memory_space=pltpu.SMEM)
@@ -37,11 +37,12 @@
     out_ref[:, rows:] = pieces_ref[EARLY % pieces_ref.shape[0]]
 
 
-def pack_kernel(pivots_ref, matrix_hbm, send_ref, table_ref, order_ref, count_ref, matrix_ref, sem):
+def pack_kernel(pivots_ref, matrix_hbm, *refs):
+    *send_refs, table_ref, order_ref, count_ref, matrix_ref, sem = refs
     nb = pivots_ref.shape[0]
     rows = matrix_ref.shape[0]
     planes = count_ref.shape[0]
-    room = send_ref.shape[0] // planes
+    rooms = [send_ref.shape[0] // planes for send_ref in send_refs]
     me = lax.axis_index("prow")
     bits = rows.bit_length() - 1
     fetch_matrix = pltpu.make_async_copy(matrix_hbm, matrix_ref, sem)
@@ -55,60 +56,68 @@
 
     lax.fori_loop(0, nb, start, 0, unroll=16)
 
+    for d in range(planes):
+        count_ref[d] = 0
+
     def exchange(j, _):
         target = pivots_ref[j]
         first = order_ref[j]
-        second = order_ref[target]
-        order_ref[j] = second
+        row = order_ref[target]
         order_ref[target] = first
-        return 0
-
-    lax.fori_loop(0, nb, exchange, 0, unroll=16)
-    for d in range(planes):
-        count_ref[d] = 0
-
-    def tally(i, _):
-        row = order_ref[i]
-        partner = order_ref[row]
+        table_ref[Table.ROW * nb + j] = row
         owner = row >> bits
         nth = count_ref[owner]
         count_ref[owner] = nth + 1
-        table_ref[Table.ROW * nb + i] = row
-        table_ref[Table.PARTNER * nb + i] = partner
-        table_ref[Table.PLACE * nb + i] = ((owner + MAIN) & (planes - 1)) * room + jnp.minimum(nth, room - 1)
-        table_ref[jnp.where(owner == me, Table.OWN * nb + nth, Table.COUNT * nb)] = i
-        return 0
-
-    lax.fori_loop(0, nb, tally, 0, unroll=16)
+        table_ref[Table.PLACE * nb + j] = (((owner + MAIN) & (planes - 1)) << 8) + nth
+        table_ref[jnp.where(owner == me, Table.OWN * nb + nth, Table.COUNT * nb)] = j
+        return 0
+
+    lax.fori_loop(0, nb, exchange, 0, unroll=16)
     table_ref[Table.COUNT * nb] = count_ref[me]
     most = count_ref[1]
     for d in range(2, planes):
         most = jnp.maximum(most, count_ref[d])
-    table_ref[Table.COUNT * nb + 1] = jnp.where(count_ref[0] + most <= room, 1, 0)
-    fetch_matrix.wait()
-
-    def give(n, _):
-        send_ref[pl.ds(n, 1), :] = matrix_ref[pl.ds(table_ref[Table.ROW * nb + table_ref[Table.OWN * nb + n]] & (rows - 1), 1), :]
-        return 0
-
-    lax.fori_loop(0, jnp.minimum(count_ref[me], room), give, 0)
-    given = send_ref[:room, :]
-    for d in range(1, planes):
-        send_ref[d * room : (d + 1) * room, :] = given
 
     @pl.when(me == 0)
     def _():
-        def hand(i, _):
-            place = table_ref[Table.PLACE * nb + i]
-            owner = table_ref[Table.ROW * nb + i] >> bits
-            away = owner > 0
-            partner = jnp.where(away, table_ref[Table.PARTNER * nb + i], 0)
-            put = 2 * ((owner + MAIN) & (planes - 1)) * room + room - 1 - place
-            put = jnp.where(away, put, MAIN * room + room - 1)
-            send_ref[pl.ds(put, 1), :] = matrix_ref[pl.ds(partner, 1), :]
+        def meet(i, _):
+            table_ref[Table.PARTNER * nb + i] = order_ref[table_ref[Table.ROW * nb + i]]
             return 0
 
-        lax.fori_loop(0, nb, hand, 0, unroll=16)
+        lax.fori_loop(0, nb, meet, 0, unroll=16)
+
+    most = count_ref[0] + most
+    level = len(rooms)
+    for n in reversed(range(len(rooms))):
+        level = jnp.where(most <= rooms[n], n, level)
+    table_ref[Table.COUNT * nb + 1] = level
+    fetch_matrix.wait()
+
+    def fill(send_ref, room):
+        def give(n, _):
+            mine = table_ref[Table.ROW * nb + table_ref[Table.OWN * nb + n]] & (rows - 1)
+            send_ref[pl.ds(n, 1), :] = matrix_ref[pl.ds(mine, 1), :]
+            return 0
+
+        lax.fori_loop(0, count_ref[me], give, 0)
+        given = send_ref[:room, :]
+        for d in range(1, planes):
+            send_ref[d * room : (d + 1) * room, :] = given
+
+        @pl.when(me == 0)
+        def _():
+            def hand(i, _):
+                place = table_ref[Table.PLACE * nb + i]
+                away = table_ref[Table.ROW * nb + i] >= rows
+                partner = jnp.where(away, table_ref[Table.PARTNER * nb + i], 0)
+                put = jnp.where(away, ((place >> 8) + 1) * room - (place & 255), (MAIN + 1) * room) - 1
+                send_ref[pl.ds(put, 1), :] = matrix_ref[pl.ds(partner, 1), :]
+                return 0
+
+            lax.fori_loop(0, nb, hand, 0, unroll=16)
+
+    for n, send_ref in enumerate(send_refs):
+        pl.when(level == n)(partial(fill, send_ref, rooms[n]))
 
 
 def slot_kernel(table_ref, matrix_ref, send_ref):
@@ -177,7 +186,10 @@
 
     def pick(d, _):
         for k in range(slots):
-            place = table_ref[Table.PLACE * nb + d * slots + k] if one_round else d * room + k
+            place = d * room + k
+            if one_round:
+                place = table_ref[Table.PLACE * nb + d * slots + k]
+                place = (place >> 8) * room + (place & 255)
             upper_ref[d, k : k + 1, :] = arrived_ref[pl.ds(place, 1), :]
         return 0
 
@@ -231,19 +243,19 @@
     planes = lax.axis_size("prow")
     slots = nb // planes
     width = factored_panel.shape[1]
-    room = min(ROUND, nb)
+    rooms = ROUNDS
     f32 = jnp.float32
     panel = factored_panel.T
     pieces = call(spread_kernel, jax.ShapeDtypeStruct((planes, width, nb), f32), [VMEM], VMEM)(panel)
     pieces = exchange(pieces, EARLY)
-    send, table = call(
+    *sends, table = call(
         pack_kernel,
         (
-            jax.ShapeDtypeStruct((planes * room, cols), f32),
+            *(jax.ShapeDtypeStruct((planes * room, cols), f32) for room in rooms),
             jax.ShapeDtypeStruct((8 * nb,), jnp.int32),
         ),
         [SMEM, HBM],
-        (VMEM, SMEM),
+        (*(VMEM for _ in rooms), SMEM),
         [
             pltpu.SMEM((rows * planes,), jnp.int32),
             pltpu.SMEM((planes,), jnp.int32),
@@ -273,11 +285,11 @@
             [pltpu.VMEM((planes, slots, cols), f32)],
         )(table, *by_rows, arrived, matrix)
 
-    def one_round(send, table, panel, pieces, matrix):
-        arrived = exchange(send.reshape(planes, room, cols), MAIN)
-        return finish(True, table, panel, pieces, arrived.reshape(planes * room, cols), matrix)
-
-    def two_rounds(send, table, panel, pieces, matrix):
+    def one_round(level, sends, table, panel, pieces, matrix):
+        arrived = exchange(sends[level].reshape(planes, rooms[level], cols), MAIN)
+        return finish(True, table, panel, pieces, arrived.reshape(planes * rooms[level], cols), matrix)
+
+    def two_rounds(sends, table, panel, pieces, matrix):
         slot = jax.ShapeDtypeStruct((planes, slots, cols), f32)
         both = jax.ShapeDtypeStruct((planes, 2 * slots, cols), f32)
         arrived = exchange(call(slot_kernel, slot, [SMEM, VMEM], VMEM)(table, matrix), 0)
@@ -285,8 +297,8 @@
         arrived = exchange(send, 0)
         return finish(False, table, panel, pieces, arrived.reshape(2 * nb, cols), matrix)
 
-    fits = table[Table.COUNT * nb + 1] == 1
-    return lax.cond(fits, one_round, two_rounds, send, table, panel, pieces, matrix)
+    forms = [*(partial(one_round, level) for level in range(len(rooms))), two_rounds]
+    return lax.switch(table[Table.COUNT * nb + 1], forms, sends, table, panel, pieces, matrix)
 
 
 def solution(mesh):

time: 76.7 us -> 76.9 us (level)
  the two profiles are of different devices: /device:TPU:58 before, /device:TPU:14 now
where the time goes in v4:
time: 76.9 us; the launch traced here: 76.6 us
  starting transfers between devices  23.5 us (31%)
  blocking collectives  23.3 us (30%)
  Pallas kernels  17.2 us (22%)
  waiting for transfers between devices  10.1 us (13%)
  local copies, waits for them, and re-layouts  1.41 us (2%)
    all_to_all x2, starting transfers between devices, exchange(): return lax.all_to_all(value, 'prow', 0, 0, axis_index_groups=order)  23.5 us
    all_gather x1, blocking collectives, finish(): gathered = lax.all_gather(pieces, 'pcol', axis=0, tiled=True)  23.3 us
    all_to_all x2, waiting for transfers between devices, exchange(): return lax.all_to_all(value, 'prow', 0, 0, axis_index_groups=order)  10.1 us
    pallas_call x1, Pallas kernels, local(): call(pack_kernel, (*(jax.ShapeDtypeStruct((planes * room, cols), f32) for...  7.67 us
    pallas_call x1, Pallas kernels, finish(): call(invert_kernel, (jax.ShapeDtypeStruct((rows, nb), f32), jax.ShapeDtyp...  4.79 us
    pallas_call x1, Pallas kernels, finish(): call(partial(update_kernel, one_round), jax.ShapeDtypeStruct((rows, cols)...  3.37 us
  transfers between devices with their start and end apart: 2, of which 2 were waited for; matrix products, arithmetic and copies ran while one was open for 1% of the time, Pallas kernels for 16%

profile of v4, /device:TPU:14, one launch (start us, length us, event | category | flops | bytes accessed | tf_op | source)
XLA Modules:
  0.0 76.6 jit_solution(4551707081570488215)
XLA Ops:
  0.0 1.4 %shard_map.41 = f32[16,8,256]{2,1,0:T(8,128)} custom-call(f32[8,512]{1,0:T(8,128)} %bitcast.10), custom_call_target="tpu_custom_call" | custom-call | tf_op jit(solution)/shard_map/pallas_call | solution.py:249
  1.4 0.0 copy-start
  1.4 0.0 copy-start.1
  1.4 15.8 %all-to-all-start.4 = ((f32[16,8,256]{2,1,0:T(8,128)}), f32[16,8,256]{2,1,0:T(8,128)S(1)}, u32[]{:S(2)}, u32[]{:S(2)}) async-start(f32[16,8,256]{2,1,0:T(8,128)} %shard_map.41), calls=%async_computation.4 | async-start | bytes 262144 | tf_op jit(solution)/shard_map/all_to_all | solution.py:237
  17.2 0.0 copy-done
  17.2 0.0 copy-start.3
  17.2 7.7 %shard_map.40 = (f32[640,256]{1,0:T(8,128)}, f32[768,256]{1,0:T(8,128)}, s32[2048]{0:T(1024)S(1)}) custom-call(s32[256]{0:T(256)S(1)} %copy-done, f32[512,256]{1,0:T(8,128)} %matrix_hbm.1), custom_call_target="tpu_custom_call" | custom-call | tf_op jit(solution)/shard_map/pallas_call | solution.py:251
  24.9 0.6 slice.3
  26.1 1.9 %all-to-all-done.4 = f32[16,8,256]{2,1,0:T(8,128)S(1)} async-done(((f32[16,8,256]{2,1,0:T(8,128)}), f32[16,8,256]{2,1,0:T(8,128)S(1)}, u32[]{:S(2)}, u32[]{:S(2)}) %all-to-all-start.4) | async-done | bytes 131104 | tf_op jit(solution)/shard_map/all_to_all | solution.py:237
  28.1 0.0 copy-done.1
  28.1 0.0 copy-done.3
  28.1 47.7 %conditional.1 = (f32[512,256]{1,0:T(8,128)S(1)}) conditional(s32[]{:T(128)} %bitcast.5, (f32[8,512]{1,0:T(8,128)S(1)}, f32[16,8,256]{2,1,0:T(8,128)S(1)}, f32[640,256]{1,0:T(8,128)}, s32[2048]{0:T(1024)S(1)}, f32[512,256]{1,0:T(8,128)S(1)}) %tuple.27, (f32[8,512]{1,0:T(8,128)S(1)}, f32[16,8,256]{2,1,0:T(8,128)S(1)}, ...), branch_computations={%region_0.0_spmd, %region_1.0_spmd, %region_2.0_spmd} | conditional | bytes 3170344 | solution.py:301
  28.1 7.7 %all-to-all-start.1 = ((f32[16,48,256]{2,1,0:T(8,128)}), f32[16,48,256]{2,1,0:T(8,128)S(1)}, u32[]{:S(2)}, u32[]{:S(2)}) async-start(f32[16,48,256]{2,1,0:T(8,128)} %bitcast.2), calls=%async_computation.1 | async-start | bytes 1572864 | tf_op jit(solution)/shard_map/cond/branch_1_fun/all_to_all | solution.py:237
  35.7 23.3 %all_gather.7.gathered_ref = f32[256,768]{1,0:T(8,128)S(1)} all-gather(f32[8,768]{1,0:T(8,128)S(1)} %branch_1_fun.3), channel_id=1, replica_groups=mesh['prow'=16,'pcol'=32] {'pcol'}, dimensions={0}, use_global_device_ids=true | all-gather | bytes 811008 | tf_op jit(solution)/shard_map/cond/branch_1_fun/all_gather | solution.py:269
  59.1 4.8 %branch_1_fun.4 = (f32[512,256]{1,0:T(8,128)S(1)}, f32[256,128]{1,0:T(8,128)S(1)}, f32[128,128]{1,0:T(8,128)S(1)}) custom-call(f32[256,768]{1,0:T(8,128)S(1)} %all_gather.7.gathered_ref), custom_call_target="tpu_custom_call" | custom-call | tf_op jit(solution)/shard_map/cond/branch_1_fun/pallas_call | solution.py:270
  63.9 8.1 %all-to-all-done.1 = f32[16,48,256]{2,1,0:T(8,128)S(1)} async-done(((f32[16,48,256]{2,1,0:T(8,128)}), f32[16,48,256]{2,1,0:T(8,128)S(1)}, u32[]{:S(2)}, u32[]{:S(2)}) %all-to-all-start.1) | async-done | bytes 786464 | tf_op jit(solution)/shard_map/cond/branch_1_fun/all_to_all | solution.py:237
  72.0 3.4 %branch_1_fun.5 = f32[512,256]{1,0:T(8,128)S(1)} custom-call(s32[2048]{0:T(1024)S(1)} %get-tuple-element.45.table_ref, f32[512,256]{1,0:T(8,128)S(1)} %get-tuple-element.48.panel_ref, f32[256,128]{1,0:T(8,128)S(1)} %get-tuple-element.49.inverse_ref, f32[128,128]{1,0:T(8,128)S(1)} %get-tuple-element.50.lower_ref, f32[768,256]{1,0:T(8,128)S(1)} %bitcast.7, ...), custom_call_target="tpu_custom_call" | custom-call | tf_op jit(solution)/shard_map/cond/branch_1_fun/pallas_call | solution.py:280
  75.8 0.0 copy-start.2
  75.8 0.8 %copy-done.2 = f32[512,256]{1,0:T(8,128)} copy-done((f32[512,256]{1,0:T(8,128)}, f32[512,256]{1,0:T(8,128)S(1)}, u32[]{:S(2)}) %copy-start.2) | copy-done | bytes 524312
  (1 shorter events, 0.0 us)
Async XLA Ops:
  1.4 15.8 %copy-start = (s32[256]{0:T(256)S(1)}, s32[256]{0:T(256)}, u32[]{:S(2)}) copy-start(s32[256]{0:T(256)} %pivots_ref.1) | copy-start | bytes 3076
  1.4 26.7 %copy-start.1 = (f32[512,256]{1,0:T(8,128)S(1)}, f32[512,256]{1,0:T(8,128)}, u32[]{:S(2)}) copy-start(f32[512,256]{1,0:T(8,128)} %matrix_hbm.1) | copy-start | bytes 1572868
  1.4 26.7 %all-to-all-start.4 = ((f32[16,8,256]{2,1,0:T(8,128)}), f32[16,8,256]{2,1,0:T(8,128)S(1)}, u32[]{:S(2)}, u32[]{:S(2)}) async-start(f32[16,8,256]{2,1,0:T(8,128)} %shard_map.41), calls=%async_computation.4 | async-start | bytes 262144 | tf_op jit(solution)/shard_map/all_to_all | solution.py:237
  17.2 10.9 %copy-start.3 = (f32[512,8]{0,1:T(8,128)S(1)}, f32[512,8]{0,1:T(8,128)}, u32[]{:S(2)}) copy-start(f32[512,8]{0,1:T(8,128)} %param.7) | copy-start | bytes 49156
  28.1 44.0 %all-to-all-start.1 = ((f32[16,48,256]{2,1,0:T(8,128)}), f32[16,48,256]{2,1,0:T(8,128)S(1)}, u32[]{:S(2)}, u32[]{:S(2)}) async-start(f32[16,48,256]{2,1,0:T(8,128)} %bitcast.2), calls=%async_computation.1 | async-start | bytes 1572864 | tf_op jit(solution)/shard_map/cond/branch_1_fun/all_to_all | solution.py:237
  75.8 0.8 %copy-start.2 = (f32[512,256]{1,0:T(8,128)}, f32[512,256]{1,0:T(8,128)S(1)}, u32[]{:S(2)}) copy-start(f32[512,256]{1,0:T(8,128)S(1)} %get-tuple-element.74) | copy-start | bytes 1572868
